TPU v7x, 32 devices: a whole 2x2x4 slice. The times are simulated.
32 devices in a mesh: groups: 2 (over y), pool: 4 (over z), tensor: 2 (over x), sub: 2 (over core).
Axes of the slice: x: 2, y: 2, z: 4, core: 2. Of those that a mesh axis runs over, the one named last changes fastest.
Arguments:
- patches: bfloat16 [1280, 8192], P(('tensor', 'sub'), ('groups', 'pool')), parts along dimension 1, may hold values from -6 to 6
- window_ids: int32 [32, 256], P(('groups', 'pool')), parts along dimension 0, may hold values from 0 to 5, never falling along the last dimension, each value on 1 to 64 neighbouring positions
- block_route: int32 [32], P('groups'), parts along dimension 0, may hold values from 0 to 3, as said below
- norm_gain: float32 [1280], P(('tensor', 'sub')), may hold values from 0.25 to 1.75
- qkv_weight: bfloat16 [3, 1280, 1280], P(None, None, ('tensor', 'sub')), may hold values from -0.15625 to 0.15625
- qkv_bias: float32 [3, 1280], P(None, ('tensor', 'sub')), may hold values from -3 to 3
- proj_weight: bfloat16 [1280, 1280], P(('tensor', 'sub')), may hold values from -0.15625 to 0.15625
- proj_bias: float32 [1280], P(('tensor', 'sub')), may hold values from -3 to 3
- merge_gain: float32 [1280], P(('tensor', 'sub')), may hold values from 0.25 to 1.75
- w1: bfloat16 [4, 1280, 2560], P(None, ('tensor', 'sub'), 'pool'), may hold values from -0.078125 to 0.078125
- b1: float32 [2560], P(('tensor', 'sub')), may hold values from -3 to 3
- w2: bfloat16 [2560, 8192], P('pool', ('tensor', 'sub')), may hold values from -0.125 to 0.125
- b2: float32 [8192], P(('tensor', 'sub')), may hold values from -2 to 2
- llm_gain: float32 [8192], P(('tensor', 'sub')), may hold values from 0.25 to 1.75
Outputs:
- image_embeds: bfloat16 [8192, 2048], P(('tensor', 'sub'), ('groups', 'pool')), parts along dimension 1
- normed_embeds: bfloat16 [8192, 2048], P(('tensor', 'sub'), ('groups', 'pool')), parts along dimension 1
There are 2 independent parts, one for each index of `groups`. A program takes and returns all parts, laid end to end along the dimension named above; an argument that names none is the same for every part. Nothing has to cross between parts.
Inputs may be any that keep to these rules, and one draw needn't show every extreme that they name: `window_ids`: window ids never fall along a block; each window holds at most 64 patches. `block_route`: at most 2 blocks of one pool group's 4 go to one pool index, and at most 4 blocks of all go to one pool index; both bounds are reached.
All inputs are finite; a program needn't handle non-finite values.
Results may differ from a plain program's by a relative error of at most 0.018.
Values may be sent and summed in bfloat16 or wider, within the bound.
A program may use at most 128 MiB of HBM per device.

v0:
```python
import jax
import jax.numpy as jnp
from jax import lax
from jax.sharding import PartitionSpec as P

HDIM = 80


EPSILON = 1e-06


def shards(
    patches,
    window_ids,
    block_route,
    norm_gain,
    qkv_weight,
    qkv_bias,
    proj_weight,
    proj_bias,
    merge_gain,
    w1,
    b1,
    w2,
    b2,
    llm_gain,
):
    feature_share, local_cols = patches.shape
    vision_width = qkv_weight.shape[1]
    groups = lax.axis_size(("tensor", "sub"))
    pool_count = lax.axis_size("pool")
    my_pool = lax.axis_index("pool")
    block_slots, block_len = window_ids.shape
    merged_rows = block_len // 4
    feats = patches.astype(jnp.float32)
    squares = lax.psum(jnp.sum(feats * feats, 0), ("tensor", "sub"))
    patch_in = (
        feats * lax.rsqrt(squares / vision_width + EPSILON)[None, :] * norm_gain[:, None]
    ).astype(jnp.bfloat16)
    weight_rows = qkv_weight
    qkv_total = jnp.einsum(
        "cio,in->con",
        weight_rows,
        lax.all_gather(patch_in, ("tensor", "sub"), axis=0, tiled=True),
        preferred_element_type=jnp.float32,
    )
    qkv = (qkv_total + qkv_bias[:, :, None]).astype(jnp.bfloat16)
    head_count = feature_share // HDIM
    qkv = qkv.reshape(3, head_count, HDIM, block_slots, block_len)
    same_window = window_ids[:, :, None] == window_ids[:, None, :]
    scores = jnp.einsum(
        "hdbi,hdbj->hbij", qkv[0], qkv[1], preferred_element_type=jnp.float32
    ) * HDIM ** (-0.5)
    scores = jnp.where(same_window[None], scores, -1e30)
    row_peak = jnp.max(scores, -1, keepdims=True)
    exponent = jnp.exp(scores - row_peak)
    attention_weights = (exponent / jnp.sum(exponent, -1, keepdims=True)).astype(jnp.bfloat16)
    context = jnp.einsum(
        "hbij,hdbj->hdbi", attention_weights, qkv[2], preferred_element_type=jnp.float32
    )
    context = context.astype(jnp.bfloat16).reshape(feature_share, local_cols)
    attn_out = lax.psum_scatter(
        jnp.einsum("hc,hn->cn", proj_weight, context, preferred_element_type=jnp.float32).astype(
            jnp.bfloat16
        ),
        ("tensor", "sub"),
        scatter_dimension=0,
        tiled=True,
    ).astype(jnp.float32)
    patch_out = (feats + attn_out + proj_bias[:, None]).astype(jnp.bfloat16)
    out_f = patch_out.astype(jnp.float32)
    merge_squares = lax.psum(jnp.sum(out_f * out_f, 0), ("tensor", "sub"))
    merge_in = (
        out_f * lax.rsqrt(merge_squares / vision_width + EPSILON)[None, :] * merge_gain[:, None]
    ).astype(jnp.bfloat16)
    merged = merge_in.reshape(feature_share, local_cols // 4, 4).transpose(2, 0, 1)
    merger_first = lax.all_gather(w1, "pool", axis=2, tiled=True)
    hidden_width = merger_first.shape[2]
    hidden_share = hidden_width // groups
    hidden_full = lax.psum(
        jnp.einsum("jfc,jfm->cm", merger_first, merged, preferred_element_type=jnp.float32).astype(
            jnp.bfloat16
        ),
        ("tensor", "sub"),
    ).astype(jnp.float32)
    hidden_pre = lax.dynamic_slice_in_dim(
        hidden_full, lax.axis_index(("tensor", "sub")) * hidden_share, hidden_share, 0
    )
    hidden = jax.nn.gelu(hidden_pre + b1[:, None], approximate=False).astype(jnp.bfloat16)
    hidden_blocks = hidden.reshape(hidden_share, block_slots, merged_rows)
    hot_groups = max(1, pool_count // 16)
    capacity_in = 2 * hot_groups + block_slots - 2
    block_total = block_route.shape[0]
    block_index = jnp.arange(block_total, dtype=jnp.int32)
    is_mine = (block_route == my_pool).astype(jnp.int32)
    count_mine = jnp.sum(is_mine)
    slot_index = jnp.arange(capacity_in, dtype=jnp.int32)
    everything = lax.all_gather(hidden_blocks, "pool", axis=1, tiled=True)
    order_rank = jnp.sum(
        is_mine[None, :] * (block_index[None, :] < block_index[:, None]).astype(jnp.int32), 1
    )
    take_select = ((is_mine[None, :] == 1) & (order_rank[None, :] == slot_index[:, None])).astype(
        jnp.bfloat16
    )
    compact = jnp.einsum(
        "kn,fnr->fkr", take_select, everything, preferred_element_type=jnp.float32
    ).astype(jnp.bfloat16)
    compact_rows = compact.reshape(hidden_share, capacity_in * merged_rows)
    merger_second = lax.all_gather(w2, "pool", axis=0, tiled=True)
    weight_rows = merger_second
    projected = jnp.einsum(
        "hc,hn->cn",
        weight_rows,
        lax.all_gather(compact_rows, ("tensor", "sub"), axis=0, tiled=True),
        preferred_element_type=jnp.float32,
    )
    live_mask = (slot_index < count_mine).astype(jnp.float32)
    live_rows = jnp.broadcast_to(live_mask[:, None], (capacity_in, merged_rows)).reshape(-1)
    image_embeds = ((projected + b2[:, None]) * live_rows[None, :]).astype(jnp.bfloat16)
    embed_f = image_embeds.astype(jnp.float32)
    embed_squares = lax.psum(jnp.sum(embed_f * embed_f, 0), ("tensor", "sub"))
    normed_embeds = (
        embed_f
        * lax.rsqrt(embed_squares / (merger_second.shape[1] * groups) + EPSILON)[None, :]
        * llm_gain[:, None]
    ).astype(jnp.bfloat16)
    return (image_embeds, normed_embeds)


def solution(mesh):
    placed = (
        P(("tensor", "sub"), ("groups", "pool")),
        P(("groups", "pool"), None),
        P("groups"),
        P(("tensor", "sub")),
        P(None, None, ("tensor", "sub")),
        P(None, ("tensor", "sub")),
        P(("tensor", "sub"), None),
        P(("tensor", "sub")),
        P(("tensor", "sub")),
        P(None, ("tensor", "sub"), "pool"),
        P(("tensor", "sub")),
        P("pool", ("tensor", "sub")),
        P(("tensor", "sub")),
        P(("tensor", "sub")),
    )
    return jax.shard_map(
        shards,
        mesh=mesh,
        in_specs=placed,
        out_specs=(
            P(("tensor", "sub"), ("groups", "pool")),
            P(("tensor", "sub"), ("groups", "pool")),
        ),
        check_vma=False,
    )
```

profile of v0, /device:TPU:9, one launch (start us, length us, event | category | flops | bytes accessed | tf_op | source)
XLA Modules:
  0.0 493.5 jit_solution(1671199201263849363)
XLA Ops:
  8.1 1.4 fusion.24
  9.5 5.7 %psum.28 = f32[1024]{0:T(1024)S(1)} all-reduce(f32[1024]{0:T(1024)S(1)} %fusion.24), channel_id=1, replica_groups=mesh['groups'=2,'pool'=4,'tensor'=2,'sub'=2] {'tensor','sub'}, use_global_device_ids=true, to_apply=%region_1.0 | all-reduce | flops 1024 | bytes 8192 | tf_op jit(solution)/shard_map/psum | solution.py:36
  15.2 2.1 fusion.26
  17.3 0.0 reduce-scatter.2.cloned.1.call-start
  17.4 0.2 broadcast_compare_fusion
  17.6 27.3 %all-gather.6.cloned.1.call-done = bf16[1280,1024]{1,0:T(8,128)(2,1)} async-done(((bf16[320,1024]{1,0:T(8,128)(2,1)}), bf16[1280,1024]{1,0:T(8,128)(2,1)}) %all-gather.6.cloned.1.call-update) | async-done | bytes 2621456 | tf_op jit(solution)/shard_map/all_gather | solution.py:44
  44.9 4.5 fusion.17
  49.3 1.2 fusion.64
  50.5 2.5 squeeze.10
  53.0 2.5 squeeze.11
  55.5 1.3 squeeze.9
  56.8 2.0 fusion.43
  58.8 1.5 fusion.65
  60.4 0.4 fusion.31
  60.8 0.3 copy.53
  61.2 0.1 copy.63
  61.3 0.7 copy-done.9
  62.0 3.1 fusion.3
  65.1 0.0 all-gather.8.cloned.1.call-start
  65.2 0.5 all-gather.8.cloned.1.call-update
  65.8 33.8 %reduce-scatter.2.cloned.1.call-done = bf16[320,1024]{1,0:T(8,128)(2,1)} async-done(((bf16[1280,1024]{1,0:T(8,128)(2,1)}), bf16[320,1024]{1,0:T(8,128)(2,1)}) %reduce-scatter.2.cloned.1.call-update) | async-done | bytes 655376 | tf_op jit(solution)/shard_map/reduce_scatter | solution.py:62
  99.6 1.4 fusion.21
  101.0 5.7 %psum.29 = f32[1024]{0:T(1024)S(1)} all-reduce(f32[1024]{0:T(1024)S(1)} %fusion.21), channel_id=1, replica_groups=mesh['groups'=2,'pool'=4,'tensor'=2,'sub'=2] {'tensor','sub'}, use_global_device_ids=true, to_apply=%region_6.7 | all-reduce | flops 1024 | bytes 8192 | tf_op jit(solution)/shard_map/psum | solution.py:72
  106.7 2.2 fusion.23
  108.9 1.4 copy.55
  110.3 1.1 reshape.49
  111.4 72.1 %all-gather.8.cloned.1.call-done = bf16[4,320,2560]{2,1,0:T(8,128)(2,1)} async-done(((bf16[4,320,640]{2,1,0:T(8,128)(2,1)}), bf16[4,320,2560]{2,1,0:T(8,128)(2,1)}) %all-gather.8.cloned.1.call-update) | async-done | bytes 6553616 | tf_op jit(solution)/shard_map/all_gather | solution.py:77
  183.5 6.1 %fusion.2 = bf16[2560,256]{0,1:T(8,128)(2,1)} fusion(bf16[4,320,2560]{2,1,0:T(8,128)(2,1)} %all-gather.8.cloned.1.call-done, bf16[4,320,256]{1,0,2:T(4,128)(2,1)} %bitcast.43), kind=kOutput, calls=%fused_computation.8 | convolution fusion | flops 1678376960 | bytes 8519680 | tf_op jit(solution)/shard_map/jfc,jfm->cm/dot_general | solution.py:81
  189.6 0.0 all-gather.10.cloned.1.call-start
  189.7 40.1 %all-reduce.2.cloned.1.call-done = bf16[2560,256]{0,1:T(8,128)(2,1)} async-done(((bf16[2560,256]{0,1:T(8,128)(2,1)}), bf16[2560,256]{0,1:T(8,128)(2,1)}) %all-reduce.2.cloned.1.call-update) | async-done | bytes 1310736 | tf_op jit(solution)/shard_map/psum | solution.py:80
  229.7 3.2 fusion.41
  232.9 0.0 all-gather.12.cloned.1.call-start
  233.0 0.6 fusion.63
  233.6 0.1 select_reduce_fusion
  233.7 30.8 %all-gather.10.cloned.1.call-done = bf16[640,16,64]{0,2,1:T(8,128)(2,1)} async-done(((bf16[640,4,64]{0,2,1:T(8,128)(2,1)}), bf16[640,16,64]{0,2,1:T(8,128)(2,1)}) %all-gather.10.cloned.1.call-update) | async-done | bytes 1310736 | tf_op jit(solution)/shard_map/all_gather | solution.py:98
  264.6 2.1 fusion.35
  266.7 0.8 copy.58
  267.6 0.5 all-gather.14.cloned.1.call-update
  268.1 0.7 compare_convert_fusion
  268.8 0.1 broadcast_in_dim.16
  268.8 0.1 mul.124
  268.9 17.4 %all-gather.12.cloned.1.call-done = bf16[2560,256]{0,1:T(8,128)(2,1)} async-done(((bf16[640,256]{0,1:T(8,128)(2,1)}), bf16[2560,256]{0,1:T(8,128)(2,1)}) %all-gather.12.cloned.1.call-update) | async-done | bytes 1310736 | tf_op jit(solution)/shard_map/all_gather | solution.py:114
  286.3 182.2 %all-gather.14.cloned.1.call-done = bf16[2560,2048]{1,0:T(8,128)(2,1)} async-done(((bf16[640,2048]{1,0:T(8,128)(2,1)}), bf16[2560,2048]{1,0:T(8,128)(2,1)}) %all-gather.14.cloned.1.call-update) | async-done | bytes 10485776 | tf_op jit(solution)/shard_map/all_gather | solution.py:109
  468.5 7.4 %fusion.10 = (f32[256]{0:T(256)S(1)}, bf16[2048,256]{0,1:T(8,128)(2,1)S(1)}) fusion(f32[256]{0:T(256)S(1)} %mul.124, f32[2048]{0:T(1024)S(1)} %copy-done.10, bf16[2560,256]{0,1:T(8,128)(2,1)} %all-gather.12.cloned.1.call-done, bf16[2560,2048]{1,0:T(8,128)(2,1)} %all-gather.14.cloned.1.call-done), kind=kOutput, calls=%fused_computation.19 | convolution fusion | flops 2687500032 | bytes 12855296 | tf_op jit(solution)/shard_map/hc,hn->cn/dot_general | solution.py:111
  475.9 5.6 %psum.31 = f32[256]{0:T(256)S(1)} all-reduce(f32[256]{0:T(256)S(1)} %get-tuple-element.17), channel_id=1, replica_groups=mesh['groups'=2,'pool'=4,'tensor'=2,'sub'=2] {'tensor','sub'}, use_global_device_ids=true, to_apply=%region_11.12 | all-reduce | flops 256 | bytes 2048 | tf_op jit(solution)/shard_map/psum | solution.py:121
  481.5 1.3 copy.59
  482.8 1.3 fusion.12
  484.1 2.3 copy.60
  (35 shorter events, 0.3 us)
Async XLA Ops:
  8.0 36.9 %copy-start = (bf16[3,1280,320]{1,2,0:T(8,128)(2,1)S(1)}, bf16[3,1280,320]{1,2,0:T(8,128)(2,1)}, u32[]{:S(2)}) copy-start(bf16[3,1280,320]{1,2,0:T(8,128)(2,1)} %param.18) | copy-start | bytes 7372804
  8.0 9.4 %copy-start.3 = (s32[4,256]{1,0:T(4,128)S(1)}, s32[4,256]{1,0:T(4,128)}, u32[]{:S(2)}) copy-start(s32[4,256]{1,0:T(4,128)} %param.15) | copy-start | bytes 12292
  8.0 36.8 %copy-start.11 = (f32[3,320]{1,0:T(4,128)S(1)}, f32[3,320]{1,0:T(4,128)}, u32[]{:S(2)}) copy-start(f32[3,320]{1,0:T(4,128)} %param.19) | copy-start | bytes 11524
  8.0 36.8 %all-gather.6.cloned.1.call-start = ((), (), s32[]{:S(2)}) async-start(), calls=%async_computation.1 | async-start | bytes 3276800 | tf_op jit(solution)/shard_map/all_gather | solution.py:44
  17.3 82.3 %reduce-scatter.2.cloned.1.call-start = ((), (), s32[]{:S(2)}) async-start(), calls=%async_computation.2 | async-start | bytes 3276800 | tf_op jit(solution)/shard_map/reduce_scatter | solution.py:62
  58.8 1.6 copy-start.2
  60.8 1.1 copy-start.9
  65.1 34.5 %copy-start.1 = (bf16[320,1024]{1,0:T(8,128)(2,1)S(1)}, bf16[320,1024]{1,0:T(8,128)(2,1)}, u32[]{:S(2)}) copy-start(bf16[320,1024]{1,0:T(8,128)(2,1)} %param.14) | copy-start | bytes 1966084
  65.1 34.5 %copy-start.5 = (f32[320]{0:T(512)S(1)}, f32[320]{0:T(512)}, u32[]{:S(2)}) copy-start(f32[320]{0:T(512)} %param.21) | copy-start | bytes 3844
  65.1 41.5 %copy-start.7 = (f32[320]{0:T(512)S(1)}, f32[320]{0:T(512)}, u32[]{:S(2)}) copy-start(f32[320]{0:T(512)} %param.22) | copy-start | bytes 3844
  65.1 118.4 %all-gather.8.cloned.1.call-start = ((), (), s32[]{:S(2)}) async-start(), calls=%async_computation.3 | async-start | bytes 8192000 | tf_op jit(solution)/shard_map/all_gather | solution.py:77
  65.7 164.0 %all-reduce.2.cloned.1.call-start = ((), (), s32[]{:S(2)}) async-start(), calls=%async_computation.4 | async-start | bytes 2621440 | tf_op jit(solution)/shard_map/psum | solution.py:80
  183.5 46.2 %copy-start.6 = (f32[640]{0:T(1024)S(1)}, f32[640]{0:T(1024)}, u32[]{:S(2)}) copy-start(f32[640]{0:T(1024)} %param.24) | copy-start | bytes 7684
  189.6 43.4 %copy-start.8 = (s32[16]{0:T(128)S(1)}, s32[16]{0:T(128)}, u32[]{:S(2)}) copy-start(s32[16]{0:T(128)} %param.16) | copy-start | bytes 196
  189.6 75.0 %all-gather.10.cloned.1.call-start = ((), (), s32[]{:S(2)}) async-start(), calls=%async_computation.5 | async-start | bytes 1638400 | tf_op jit(solution)/shard_map/all_gather | solution.py:98
  232.9 53.3 %all-gather.12.cloned.1.call-start = ((), (), s32[]{:S(2)}) async-start(), calls=%async_computation.6 | async-start | bytes 1638400 | tf_op jit(solution)/shard_map/all_gather | solution.py:114
  266.7 201.8 %copy-start.10 = (f32[2048]{0:T(1024)S(1)}, f32[2048]{0:T(1024)}, u32[]{:S(2)}) copy-start(f32[2048]{0:T(1024)} %param.26) | copy-start | bytes 24580
  267.5 201.0 %all-gather.14.cloned.1.call-start = ((), (), s32[]{:S(2)}) async-start(), calls=%async_computation.7 | async-start | bytes 13107200 | tf_op jit(solution)/shard_map/all_gather | solution.py:109
  475.9 6.9 %copy-start.4 = (f32[2048]{0:T(1024)S(1)}, f32[2048]{0:T(1024)}, u32[]{:S(2)}) copy-start(f32[2048]{0:T(1024)} %param.27) | copy-start | bytes 24580
Sparse Core Ops, SparseCore 0:
  17.4 27.3 all-gather.5
  65.2 34.2 reduce-scatter.1
  189.7 39.9 all-reduce.1
  267.6 18.5 all-gather.11
  287.8 180.6 all-gather.13
Sparse Core Ops, SparseCore 1:
  67.3 116.2 all-gather.7
  233.0 31.5 all-gather.9
where the time goes:
time: 500 us; the launch traced here: 493 us
  waiting for transfers between devices  405 us (81%)
  matrix products  25.6 us (5%)
  blocking collectives  17 us (3%)
  local copies, waits for them, and re-layouts  15.6 us (3%)
  between operations  15.4 us (3%)
  other arithmetic  14.7 us (3%)
    all_gather x1, waiting for transfers between devices, shards(): merger_second = lax.all_gather(w2, 'pool', axis=0, tiled=True)  182 us
    all_gather x1, waiting for transfers between devices, shards(): merger_first = lax.all_gather(w1, 'pool', axis=2, tiled=True)  72.1 us
    psum x1, waiting for transfers between devices, shards(): lax.psum(jnp.einsum('jfc,jfm->cm', merger_first, merged, preferred_elemen...  40.1 us
    reduce_scatter x1, waiting for transfers between devices, shards(): lax.psum_scatter(jnp.einsum('hc,hn->cn', proj_weight, context, preferred_...  33.8 us
    all_gather x1, waiting for transfers between devices, shards(): everything = lax.all_gather(hidden_blocks, 'pool', axis=1, tiled=True)  30.8 us
    all_gather x1, waiting for transfers between devices, shards(): lax.all_gather(patch_in, ('tensor', 'sub'), axis=0, tiled=True)  27.3 us
    all_gather x1, waiting for transfers between devices, shards(): lax.all_gather(compact_rows, ('tensor', 'sub'), axis=0, tiled=True)  17.4 us
  transfers between devices with their start and end apart: 7, of which 7 were waited for; matrix products, arithmetic and copies ran while one was open for 2% of the time, Pallas kernels for 0%

commit v1 on v0

--- a/solution.py
+++ b/solution.py
@@ -74,46 +74,37 @@
         out_f * lax.rsqrt(merge_squares / vision_width + EPSILON)[None, :] * merge_gain[:, None]
     ).astype(jnp.bfloat16)
     merged = merge_in.reshape(feature_share, local_cols // 4, 4).transpose(2, 0, 1)
-    merger_first = lax.all_gather(w1, "pool", axis=2, tiled=True)
-    hidden_width = merger_first.shape[2]
-    hidden_share = hidden_width // groups
+    merged_all = lax.all_gather(merged, "pool", axis=2, tiled=True)
+    hidden_share = w1.shape[2]
     hidden_full = lax.psum(
-        jnp.einsum("jfc,jfm->cm", merger_first, merged, preferred_element_type=jnp.float32).astype(
+        jnp.einsum("jfc,jfm->cm", w1, merged_all, preferred_element_type=jnp.float32).astype(
             jnp.bfloat16
         ),
         ("tensor", "sub"),
     ).astype(jnp.float32)
-    hidden_pre = lax.dynamic_slice_in_dim(
-        hidden_full, lax.axis_index(("tensor", "sub")) * hidden_share, hidden_share, 0
-    )
-    hidden = jax.nn.gelu(hidden_pre + b1[:, None], approximate=False).astype(jnp.bfloat16)
-    hidden_blocks = hidden.reshape(hidden_share, block_slots, merged_rows)
+    bias_all = lax.all_gather(b1, ("tensor", "sub"), axis=0, tiled=True)
+    bias_mine = lax.dynamic_slice_in_dim(bias_all, my_pool * hidden_share, hidden_share, 0)
+    hidden = jax.nn.gelu(hidden_full + bias_mine[:, None], approximate=False).astype(jnp.bfloat16)
+    block_total = block_route.shape[0]
+    hidden_blocks = hidden.reshape(hidden_share, block_total, merged_rows)
     hot_groups = max(1, pool_count // 16)
     capacity_in = 2 * hot_groups + block_slots - 2
-    block_total = block_route.shape[0]
-    block_index = jnp.arange(block_total, dtype=jnp.int32)
-    is_mine = (block_route == my_pool).astype(jnp.int32)
-    count_mine = jnp.sum(is_mine)
+    pool_index = jnp.arange(pool_count, dtype=jnp.int32)
+    goes = (block_route[None, :] == pool_index[:, None]).astype(jnp.int32)
+    rank = jnp.cumsum(goes, 1) - goes
     slot_index = jnp.arange(capacity_in, dtype=jnp.int32)
-    everything = lax.all_gather(hidden_blocks, "pool", axis=1, tiled=True)
-    order_rank = jnp.sum(
-        is_mine[None, :] * (block_index[None, :] < block_index[:, None]).astype(jnp.int32), 1
-    )
-    take_select = ((is_mine[None, :] == 1) & (order_rank[None, :] == slot_index[:, None])).astype(
-        jnp.bfloat16
-    )
-    compact = jnp.einsum(
-        "kn,fnr->fkr", take_select, everything, preferred_element_type=jnp.float32
+    select = (
+        (goes[:, None, :] == 1) & (rank[:, None, :] == slot_index[None, :, None])
     ).astype(jnp.bfloat16)
-    compact_rows = compact.reshape(hidden_share, capacity_in * merged_rows)
-    merger_second = lax.all_gather(w2, "pool", axis=0, tiled=True)
-    weight_rows = merger_second
-    projected = jnp.einsum(
-        "hc,hn->cn",
-        weight_rows,
-        lax.all_gather(compact_rows, ("tensor", "sub"), axis=0, tiled=True),
-        preferred_element_type=jnp.float32,
-    )
+    routed = jnp.einsum(
+        "qkn,fnr->fqkr", select, hidden_blocks, preferred_element_type=jnp.float32
+    ).astype(jnp.bfloat16)
+    routed = routed.reshape(hidden_share, pool_count, capacity_in * merged_rows)
+    partial = jnp.einsum("hc,hqn->qcn", w2, routed, preferred_element_type=jnp.float32)
+    projected = lax.psum_scatter(
+        partial.astype(jnp.bfloat16), "pool", scatter_dimension=0, tiled=True
+    )[0].astype(jnp.float32)
+    count_mine = jnp.sum((block_route == my_pool).astype(jnp.int32))
     live_mask = (slot_index < count_mine).astype(jnp.float32)
     live_rows = jnp.broadcast_to(live_mask[:, None], (capacity_in, merged_rows)).reshape(-1)
     image_embeds = ((projected + b2[:, None]) * live_rows[None, :]).astype(jnp.bfloat16)
@@ -121,7 +112,7 @@
     embed_squares = lax.psum(jnp.sum(embed_f * embed_f, 0), ("tensor", "sub"))
     normed_embeds = (
         embed_f
-        * lax.rsqrt(embed_squares / (merger_second.shape[1] * groups) + EPSILON)[None, :]
+        * lax.rsqrt(embed_squares / (w2.shape[1] * groups) + EPSILON)[None, :]
         * llm_gain[:, None]
     ).astype(jnp.bfloat16)
     return (image_embeds, normed_embeds)

time: 500 us -> 328 us (0.66)
  waiting for transfers between devices: 405 us -> 224 us
  other arithmetic: 14.7 us -> 22.4 us
  blocking collectives: 17 us -> 22.8 us
    all_gather x4 -> x1, waiting for transfers between devices: 303 us -> 53 us  [shards(): merged_all = lax.all_gather(merged, 'pool', axis=2, tiled=True)]
    reduce_scatter x0 -> x1, waiting for transfers between devices: none -> 75.5 us  [shards(): lax.psum_scatter(partial.astype(jnp.bfloat16), 'pool', scatter_dimension=...]
    psum x1, waiting for transfers between devices: 40.1 us -> 33.9 us  [shards(): lax.psum(jnp.einsum('jfc,jfm->cm', w1, merged_all, preferred_element_type...]
    all_gather x0 -> x1, blocking collectives: none -> 5.79 us  [shards(): bias_all = lax.all_gather(b1, ('tensor', 'sub'), axis=0, tiled=True)]
  transfers between devices with their start and end apart: 7 -> 5, of which waited for: 7 -> 5; matrix products, arithmetic and copies ran while one was open for 2% -> 1% of each run, Pallas kernels for 0% -> 0%
where the time goes in v1:
time: 328 us; the launch traced here: 324 us
  waiting for transfers between devices  224 us (68%)
  blocking collectives  22.8 us (7%)
  other arithmetic  22.4 us (7%)
  matrix products  22.4 us (7%)
  local copies, waits for them, and re-layouts  18.3 us (6%)
  between operations  14 us (4%)
    reduce_scatter x1, waiting for transfers between devices, shards(): lax.psum_scatter(partial.astype(jnp.bfloat16), 'pool', scatter_dimension=...  75.5 us
    all_gather x1, waiting for transfers between devices, shards(): merged_all = lax.all_gather(merged, 'pool', axis=2, tiled=True)  53 us
    reduce_scatter x1, waiting for transfers between devices, shards(): lax.psum_scatter(jnp.einsum('hc,hn->cn', proj_weight, context, preferred_...  34.4 us
    psum x1, waiting for transfers between devices, shards(): lax.psum(jnp.einsum('jfc,jfm->cm', w1, merged_all, preferred_element_type...  33.9 us
    all_gather x1, waiting for transfers between devices, shards(): lax.all_gather(patch_in, ('tensor', 'sub'), axis=0, tiled=True)  27.3 us
    convert_element_type x1, other arithmetic, shards(): jax.nn.gelu(hidden_full + bias_mine[:, None], approximate=False)  6.85 us
  transfers between devices with their start and end apart: 5, of which 5 were waited for; matrix products, arithmetic and copies ran while one was open for 1% of the time, Pallas kernels for 0%

profile of v1, /device:TPU:9, one launch (start us, length us, event | category | flops | bytes accessed | tf_op | source)
XLA Modules:
  0.0 324.5 jit_solution(15245536858418733573)
XLA Ops:
  7.2 1.4 fusion.37
  8.6 5.7 %psum.28 = f32[1024]{0:T(1024)S(1)} all-reduce(f32[1024]{0:T(1024)S(1)} %fusion.37), channel_id=1, replica_groups=mesh['groups'=2,'pool'=4,'tensor'=2,'sub'=2] {'tensor','sub'}, use_global_device_ids=true, to_apply=%region_1.0 | all-reduce | flops 1024 | bytes 8192 | tf_op jit(solution)/shard_map/psum | solution.py:36
  14.3 2.1 fusion.39
  16.5 0.0 reduce-scatter.3.cloned.1.call-start
  16.5 0.2 broadcast_compare_fusion
  16.8 27.3 %all-gather.4.cloned.1.call-done = bf16[1280,1024]{1,0:T(8,128)(2,1)} async-done(((bf16[320,1024]{1,0:T(8,128)(2,1)}), bf16[1280,1024]{1,0:T(8,128)(2,1)}) %all-gather.4.cloned.1.call-update) | async-done | bytes 2621456 | tf_op jit(solution)/shard_map/all_gather | solution.py:44
  44.0 5.2 %fusion.28 = bf16[3,320,1024]{2,1,0:T(8,128)(2,1)S(1)} fusion(f32[3,320]{1,0:T(4,128)S(1)} %copy-done.11, bf16[3,1280,320]{1,2,0:T(8,128)(2,1)} %param.18, bf16[1280,1024]{1,0:T(8,128)(2,1)} %all-gather.4.cloned.1.call-done), kind=kOutput, calls=%fused_computation.47 | convolution fusion | flops 2518548480 | bytes 7048960 | tf_op jit(solution)/shard_map/cio,in->con/dot_general | solution.py:41
  49.2 1.2 fusion.60
  50.4 2.5 squeeze.11
  52.9 2.5 squeeze.12
  55.4 1.3 squeeze.10
  56.7 2.0 fusion.45
  58.7 1.5 fusion.61
  60.3 0.4 fusion.43
  60.7 0.3 copy.41
  61.1 0.1 copy.54
  61.2 0.7 copy-done.10
  61.9 3.1 fusion.1
  65.0 0.0 all-gather.6.cloned.1.call-start
  65.0 34.4 %reduce-scatter.3.cloned.1.call-done = bf16[320,1024]{1,0:T(8,128)(2,1)} async-done(((bf16[1280,1024]{1,0:T(8,128)(2,1)}), bf16[320,1024]{1,0:T(8,128)(2,1)}) %reduce-scatter.3.cloned.1.call-update) | async-done | bytes 655376 | tf_op jit(solution)/shard_map/reduce_scatter | solution.py:62
  99.4 1.4 fusion.34
  100.8 5.7 %psum.29 = f32[1024]{0:T(1024)S(1)} all-reduce(f32[1024]{0:T(1024)S(1)} %fusion.34), channel_id=1, replica_groups=mesh['groups'=2,'pool'=4,'tensor'=2,'sub'=2] {'tensor','sub'}, use_global_device_ids=true, to_apply=%region_6.7 | all-reduce | flops 1024 | bytes 8192 | tf_op jit(solution)/shard_map/psum | solution.py:72
  106.5 2.2 fusion.36
  108.8 1.4 copy.43
  110.2 1.1 reshape.100
  111.3 2.1 copy.44
  113.5 0.2 all-reduce.2.cloned.1.call-start
  113.7 53.0 %all-gather.6.cloned.1.call-done = bf16[4,320,1024]{2,1,0:T(8,128)(2,1)} async-done(((bf16[4,320,256]{2,1,0:T(8,128)(2,1)}), bf16[4,320,1024]{2,1,0:T(8,128)(2,1)}) %all-gather.6.cloned.1.call-update) | async-done | bytes 2621456 | tf_op jit(solution)/shard_map/all_gather | solution.py:77
  166.8 5.6 %fusion.32 = bf16[640,1024]{0,1:T(8,128)(2,1)} fusion(bf16[4,320,1024]{2,1,0:T(8,128)(2,1)} %all-gather.6.cloned.1.call-done, bf16[4,320,640]{2,1,0:T(8,128)(2,1)} %param.23), kind=kOutput, calls=%fused_computation.55 | convolution fusion | flops 1678376960 | bytes 5570560 | tf_op jit(solution)/shard_map/jfc,jfm->cm/dot_general | solution.py:80
  172.3 0.0 reduce-scatter.5.cloned.1.call-start
  172.4 5.8 %all-gather = f32[4,1,640]{2,1,0:T(1,128)S(1)} all-gather(f32[1,1,640]{2,1,0:T(1,128)S(1)} %reshape.104), channel_id=1, replica_groups=mesh['groups'=2,'pool'=4,'tensor'=2,'sub'=2] {'tensor','sub'}, dimensions={0}, use_global_device_ids=true | all-gather | bytes 12800 | tf_op jit(solution)/shard_map/all_gather | solution.py:85
  178.3 0.2 reduce_window_sum.11
  178.5 0.1 dynamic_slice.3
  178.6 33.9 %all-reduce.2.cloned.1.call-done = bf16[640,1024]{0,1:T(8,128)(2,1)} async-done(((bf16[640,1024]{0,1:T(8,128)(2,1)}), bf16[640,1024]{0,1:T(8,128)(2,1)}) %all-reduce.2.cloned.1.call-update) | async-done | bytes 1310736 | tf_op jit(solution)/shard_map/psum | solution.py:79
  212.5 6.8 %fusion.5 = bf16[640,1024]{0,1:T(8,128)(2,1)S(1)} fusion(bf16[640,1024]{0,1:T(8,128)(2,1)} %all-reduce.2.cloned.1.call-done, f32[640]{0:T(1024)S(1)} %dynamic_slice.3), kind=kLoop, calls=%fused_computation.14 | loop fusion | flops 43909120 | bytes 2624000 | tf_op jit(solution)/shard_map/convert_element_type | solution.py:87
  219.3 1.1 fusion.31
  220.4 0.3 copy.46
  220.7 5.0 %convert_bitcast_fusion = bf16[4,2048,256]{1,2,0:T(8,128)(2,1)} fusion(bf16[640,4,256]{0,2,1:T(8,128)(2,1)S(1)} %bitcast.50, bf16[640,2048]{1,0:T(8,128)(2,1)S(1)} %copy-done), kind=kOutput, calls=%fused_computation.1 | convolution fusion | flops 2686451712 | bytes 8126464 | tf_op jit(solution)/shard_map/hc,hqn->qcn/dot_general | solution.py:103
  225.7 0.6 fusion.56
  226.4 0.6 compare_convert_fusion
  227.0 0.1 broadcast_in_dim.16
  227.1 0.1 mul.109
  227.2 75.5 %reduce-scatter.5.cloned.1.call-done = bf16[1,2048,256]{1,2,0:T(8,128)(2,1)} async-done(((bf16[4,2048,256]{1,2,0:T(8,128)(2,1)}), bf16[1,2048,256]{1,2,0:T(8,128)(2,1)}) %reduce-scatter.5.cloned.1.call-update) | async-done | bytes 1048592 | tf_op jit(solution)/shard_map/reduce_scatter | solution.py:104
  302.7 2.6 fusion.19
  305.3 5.6 %psum.31 = f32[256]{0:T(256)S(1)} all-reduce(f32[256]{0:T(256)S(1)} %get-tuple-element.8), channel_id=1, replica_groups=mesh['groups'=2,'pool'=4,'tensor'=2,'sub'=2] {'tensor','sub'}, use_global_device_ids=true, to_apply=%region_12.13 | all-reduce | flops 256 | bytes 2048 | tf_op jit(solution)/shard_map/psum | solution.py:112
  310.9 2.3 copy.47
  313.2 2.5 fusion.21
  315.7 2.3 copy.48
  (37 shorter events, 0.3 us)
Async XLA Ops:
  7.2 213.6 %copy-start = (bf16[640,2048]{1,0:T(8,128)(2,1)S(1)}, bf16[640,2048]{1,0:T(8,128)(2,1)}, u32[]{:S(2)}) copy-start(bf16[640,2048]{1,0:T(8,128)(2,1)} %param.25) | copy-start | bytes 7864324
  7.2 9.4 %copy-start.3 = (s32[4,256]{1,0:T(4,128)S(1)}, s32[4,256]{1,0:T(4,128)}, u32[]{:S(2)}) copy-start(s32[4,256]{1,0:T(4,128)} %param.15) | copy-start | bytes 12292
  7.2 36.8 %copy-start.11 = (f32[3,320]{1,0:T(4,128)S(1)}, f32[3,320]{1,0:T(4,128)}, u32[]{:S(2)}) copy-start(f32[3,320]{1,0:T(4,128)} %param.19) | copy-start | bytes 11524
  7.2 36.8 %all-gather.4.cloned.1.call-start = ((), (), s32[]{:S(2)}) async-start(), calls=%async_computation.2 | async-start | bytes 3276800 | tf_op jit(solution)/shard_map/all_gather | solution.py:44
  16.5 82.9 %reduce-scatter.3.cloned.1.call-start = ((), (), s32[]{:S(2)}) async-start(), calls=%async_computation.3 | async-start | bytes 3276800 | tf_op jit(solution)/shard_map/reduce_scatter | solution.py:62
  58.7 1.6 copy-start.2
  60.7 1.1 copy-start.10
  65.0 34.4 %copy-start.1 = (bf16[320,1024]{1,0:T(8,128)(2,1)S(1)}, bf16[320,1024]{1,0:T(8,128)(2,1)}, u32[]{:S(2)}) copy-start(bf16[320,1024]{1,0:T(8,128)(2,1)} %param.14) | copy-start | bytes 1966084
  65.0 34.4 %copy-start.6 = (f32[320]{0:T(512)S(1)}, f32[320]{0:T(512)}, u32[]{:S(2)}) copy-start(f32[320]{0:T(512)} %param.21) | copy-start | bytes 3844
  65.0 41.6 %copy-start.9 = (f32[320]{0:T(512)S(1)}, f32[320]{0:T(512)}, u32[]{:S(2)}) copy-start(f32[320]{0:T(512)} %param.22) | copy-start | bytes 3844
  65.0 101.8 %all-gather.6.cloned.1.call-start = ((), (), s32[]{:S(2)}) async-start(), calls=%async_computation.4 | async-start | bytes 3276800 | tf_op jit(solution)/shard_map/all_gather | solution.py:77
  113.5 58.9 %copy-start.7 = (f32[640]{0:T(1024)S(1)}, f32[640]{0:T(1024)}, u32[]{:S(2)}) copy-start(f32[640]{0:T(1024)} %param.24) | copy-start | bytes 7684
  113.5 64.8 %copy-start.8 = (s32[16]{0:T(128)S(1)}, s32[16]{0:T(128)}, u32[]{:S(2)}) copy-start(s32[16]{0:T(128)} %param.16) | copy-start | bytes 196
  113.5 99.0 %all-reduce.2.cloned.1.call-start = ((), (), s32[]{:S(2)}) async-start(), calls=%async_computation.5 | async-start | bytes 2621440 | tf_op jit(solution)/shard_map/psum | solution.py:79
  172.3 130.4 %reduce-scatter.5.cloned.1.call-start = ((), (), s32[]{:S(2)}) async-start(), calls=%async_computation.6 | async-start | bytes 5242880 | tf_op jit(solution)/shard_map/reduce_scatter | solution.py:104
  225.7 77.0 %copy-start.4 = (f32[2048]{0:T(1024)S(1)}, f32[2048]{0:T(1024)}, u32[]{:S(2)}) copy-start(f32[2048]{0:T(1024)} %param.26) | copy-start | bytes 24580
  225.7 87.5 %copy-start.5 = (f32[2048]{0:T(1024)S(1)}, f32[2048]{0:T(1024)}, u32[]{:S(2)}) copy-start(f32[2048]{0:T(1024)} %param.27) | copy-start | bytes 24580
Sparse Core Ops, SparseCore 0:
  16.6 27.3 all-gather.3
  65.1 34.2 reduce-scatter.2
  113.6 53.1 all-gather.5
  172.5 39.9 all-reduce.1
  225.8 76.8 reduce-scatter.4

commit v2 on v1

--- a/solution.py
+++ b/solution.py
@@ -1,6 +1,10 @@
+import functools
+
 import jax
 import jax.numpy as jnp
 from jax import lax
+from jax.experimental import pallas as pl
+from jax.experimental.pallas import tpu as pltpu
 from jax.sharding import PartitionSpec as P
 
 HDIM = 80
@@ -118,6 +122,420 @@
     return (image_embeds, normed_embeds)
 
 
+def fused_kernel(
+    vision_width, model_width, patches, ids_row, tall, fcols, small, qkv_w, pw, w1, w2, lcols, live,
+    img, nrm,
+    xall, sall, pwall, gcol, xin, qkv, ctxall, zall, pbuf, rsib, csum, rx, hid, rt, obuf, rup, rdn,
+    sq, sq2, acc_ref,
+    x_send, x_recv, c_send, c_recv, s_send, s_recv, w_send, w_recv, q_send, q_recv,
+    z_send, z_recv, h1_send, h1_recv, h2_send, h2_recv, h3_send, h3_recv,
+    o_send, u_recv, d_recv, l_send, l_recv,
+):
+    f32, bf16 = jnp.float32, jnp.bfloat16
+    feat, cols = patches.shape
+    half_cols = cols // 2
+    blocks, block_len = ids_row.shape
+    heads = feat // HDIM
+    share = w1.shape[2]
+    hs = share // 2
+    p, tx, sc = lax.axis_index("pool"), lax.axis_index("tensor"), lax.axis_index("sub")
+    me, xt, st, dt = tx * 2 + sc, (1 - tx) * 2 + sc, tx * 2 + 1 - sc, (1 - tx) * 2 + 1 - sc
+    xp, sib, diag = {"tensor": 1 - tx}, {"sub": 1 - sc}, {"tensor": 1 - tx, "sub": 1 - sc}
+    top = zall.shape[0] - 1
+
+    def rcopy(src, dst, ss, rs, dev):
+        return pltpu.make_async_remote_copy(
+            src_ref=src, dst_ref=dst, send_sem=ss, recv_sem=rs, device_id=dev,
+            device_id_type=pl.DeviceIdType.MESH,
+        )
+
+    barrier = pltpu.get_barrier_semaphore()
+    for dev in (xp, sib, diag):
+        pl.semaphore_signal(barrier, inc=1, device_id=dev, device_id_type=pl.DeviceIdType.MESH)
+
+    @pl.when(p > 0)
+    def _():
+        pl.semaphore_signal(
+            barrier, inc=1, device_id={"pool": p - 1}, device_id_type=pl.DeviceIdType.MESH
+        )
+
+    @pl.when(p < top)
+    def _():
+        pl.semaphore_signal(
+            barrier, inc=1, device_id={"pool": p + 1}, device_id_type=pl.DeviceIdType.MESH
+        )
+
+    for pair in range(2):
+        xall[pair, me] = patches[:, pair * half_cols : (pair + 1) * half_cols]
+    sall[me] = small[...]
+    pwall[me] = pw[me]
+    pl.semaphore_wait(barrier, 3 + (p + top - 1) // top + (2 * top - p - 1) // top)
+
+    def gather_start(buf, pair, ssem, rsem):
+        own = buf.at[pair, me]
+        rcopy(own, own, ssem.at[pair, 0], rsem.at[pair, me], xp).start()
+        rcopy(own, own, ssem.at[pair, 1], rsem.at[pair, me], sib).start()
+
+    def gather_finish(buf, pair, ssem, rsem):
+        other = buf.at[pair, xt]
+        fwd = rcopy(other, other, ssem.at[pair, 2], rsem.at[pair, xt], sib)
+        fwd.wait_recv()
+        fwd.start()
+        for slot in (st, dt):
+            rcopy(other, buf.at[pair, slot], ssem.at[pair, 2], rsem.at[pair, slot], sib).wait_recv()
+
+    def gather_drain(buf, pair, ssem, rsem):
+        for k in range(3):
+            rcopy(buf.at[pair, me], buf.at[pair, me], ssem.at[pair, k], rsem.at[pair, me], sib).wait_send()
+
+    peers = ((xp, xt), (sib, st), (diag, dt))
+    for k, (dev, _t) in enumerate(peers):
+        rcopy(sall.at[me], sall.at[me], s_send.at[k], s_recv.at[me], dev).start()
+    gather_start(xall, 0, x_send, x_recv)
+    gather_start(xall, 1, x_send, x_recv)
+    for k, (dev, t) in enumerate(peers):
+        rcopy(pw.at[t], pwall.at[me], w_send.at[k], w_recv.at[me], dev).start()
+    for k, (dev, t) in enumerate(peers):
+        rcopy(sall.at[t], sall.at[t], s_send.at[k], s_recv.at[t], dev).wait_recv()
+
+    rows = lax.broadcasted_iota(jnp.int32, (feat, feat), 0)
+    lanes = lax.broadcasted_iota(jnp.int32, (feat, feat), 1)
+    for t in range(4):
+        gcol[t] = jnp.sum(jnp.where(rows == lanes, sall[t, 0:1, :feat], 0.0), 1, keepdims=True)
+
+    def dot0(a, b):
+        return lax.dot_general(a, b, (((0,), (0,)), ((), ())), preferred_element_type=f32)
+
+    per_pair = blocks // 2
+    for pair in range(2):
+        gather_finish(xall, pair, x_send, x_recv)
+        total = jnp.zeros((1, half_cols), f32)
+        for t in range(4):
+            v = xall[pair, t].astype(f32)
+            total += jnp.sum(v * v, 0, keepdims=True)
+        inv = lax.rsqrt(total / vision_width + EPSILON)
+        for t in range(4):
+            xin[t * feat : (t + 1) * feat] = (
+                xall[pair, t].astype(f32) * inv * gcol[t]
+            ).astype(bf16)
+        for c in range(3):
+            qkv[c] = (dot0(qkv_w[c], xin[...]) + fcols[:, c : c + 1]).astype(bf16)
+        for bb in range(per_pair):
+            b = pair * per_pair + bb
+            lo = bb * block_len
+            same = tall[b * block_len : (b + 1) * block_len, 0:1] == ids_row[b : b + 1, :]
+
+            def head(h, carry):
+                r = pl.ds(pl.multiple_of(h * HDIM, HDIM), HDIM)
+                q = qkv[0, r, lo : lo + block_len]
+                k = qkv[1, r, lo : lo + block_len]
+                v = qkv[2, r, lo : lo + block_len]
+                scores = jnp.where(same, dot0(k, q) * HDIM ** (-0.5), -1e30)
+                e = jnp.exp(scores - jnp.max(scores, 0, keepdims=True))
+                a = (e / jnp.sum(e, 0, keepdims=True)).astype(bf16)
+                ctxall[pair, me, r, lo : lo + block_len] = jnp.dot(
+                    v, a, preferred_element_type=f32
+                ).astype(bf16)
+                return carry
+
+            lax.fori_loop(0, heads, head, 0)
+        gather_start(ctxall, pair, c_send, c_recv)
+
+    for k, (dev, t) in enumerate(peers):
+        rcopy(pw.at[t], pwall.at[t], w_send.at[k], w_recv.at[t], dev).wait_recv()
+
+    for pair in range(2):
+        gather_finish(ctxall, pair, c_send, c_recv)
+        total = patches[:, pair * half_cols : (pair + 1) * half_cols].astype(f32) + fcols[:, 3:4]
+        for t in range(4):
+            total += (
+                jnp.dot(pwall[t], ctxall[pair, t], preferred_element_type=f32)
+                .astype(bf16)
+                .astype(f32)
+            )
+        out = total.astype(bf16).astype(f32)
+        sq[pair, me] = jnp.broadcast_to(jnp.sum(out * out, 0, keepdims=True), (8, half_cols))
+        for k, (dev, t) in enumerate(peers):
+            rcopy(sq.at[pair, me], sq.at[pair, me], q_send.at[pair, k], q_recv.at[pair, me], dev).start()
+        for k, (dev, t) in enumerate(peers):
+            rcopy(sq.at[pair, t], sq.at[pair, t], q_send.at[pair, k], q_recv.at[pair, t], dev).wait_recv()
+        squares = sq[pair, 0, 0:1] + sq[pair, 1, 0:1] + sq[pair, 2, 0:1] + sq[pair, 3, 0:1]
+        merge_in = (
+            out * lax.rsqrt(squares / vision_width + EPSILON) * fcols[:, 4:5]
+        ).astype(bf16)
+        n_i = lax.broadcasted_iota(jnp.int32, (half_cols, half_cols // 4), 0)
+        m_i = lax.broadcasted_iota(jnp.int32, (half_cols, half_cols // 4), 1)
+        for j in range(4):
+            pick = jnp.where(n_i == 4 * m_i + j, 1.0, 0.0).astype(bf16)
+            zall[p, pair, j] = jnp.dot(merge_in, pick, preferred_element_type=f32).astype(bf16)
+        own = zall.at[p, pair]
+
+        @pl.when(p < top)
+        def _():
+            rcopy(own, own, z_send.at[0, p, pair], z_recv.at[p, pair], {"pool": p + 1}).start()
+
+        @pl.when(p > 0)
+        def _():
+            rcopy(own, own, z_send.at[1, p, pair], z_recv.at[p, pair], {"pool": p - 1}).start()
+
+    rows_h = lax.broadcasted_iota(jnp.int32, (hs, hs), 0)
+    lanes_h = lax.broadcasted_iota(jnp.int32, (hs, hs), 1)
+    base = small.shape[1] - share
+    b1_lo = sall[p, 0:1, base : base + hs]
+    b1_hi = sall[p, 0:1, base + hs : base + share]
+    b1_row = jnp.where(sc == 0, b1_lo, b1_hi)
+    b1_col = jnp.sum(jnp.where(rows_h == lanes_h, b1_row, 0.0), 1, keepdims=True)
+    acc_ref[:hs, 0:1] = b1_col
+
+    places = 2 * top + 1
+    width = half_cols // 4
+
+    def place(k):
+        pair, kk = k // places, k % places
+        step = (kk + 1) // 2
+        return pair, p + step * (1 - 2 * (kk % 2))
+
+    def on_chunk(k, fn):
+        pair, src = place(k)
+
+        @pl.when((k >= 0) & (k < 2 * places) & (src >= 0) & (src <= top))
+        def _():
+            fn(pair, src)
+
+    def step1(pair, src):
+        chunk = zall.at[src, pair]
+
+        @pl.when(src != p)
+        def _():
+            rcopy(chunk, chunk, z_send.at[0, src, pair], z_recv.at[src, pair], sib).wait_recv()
+
+        @pl.when((src < p) & (p < top))
+        def _():
+            rcopy(chunk, chunk, z_send.at[0, src, pair], z_recv.at[src, pair], {"pool": p + 1}).start()
+
+        @pl.when((src > p) & (p > 0))
+        def _():
+            rcopy(chunk, chunk, z_send.at[1, src, pair], z_recv.at[src, pair], {"pool": p - 1}).start()
+
+        c = src * 2 + pair
+        total = dot0(w1[0], zall[src, pair, 0])
+        for j in range(1, 4):
+            total += dot0(w1[j], zall[src, pair, j])
+        pbuf[c, 0] = total[:hs].astype(bf16)
+        pbuf[c, 1] = total[hs:].astype(bf16)
+        rcopy(pbuf.at[c, 1 - sc], rsib.at[c], h1_send.at[c], h1_recv.at[c], sib).start()
+
+    def step2(pair, src):
+        c = src * 2 + pair
+        rcopy(pbuf.at[c, 1 - sc], rsib.at[c], h1_send.at[c], h1_recv.at[c], sib).wait()
+        csum[c] = (pbuf[c, sc].astype(f32) + rsib[c].astype(f32)).astype(bf16)
+        rcopy(csum.at[c], rx.at[c], h2_send.at[c], h2_recv.at[c], xp).start()
+
+    def hid_copy(c):
+        dst = hid.at[sc, :, pl.ds(pl.multiple_of(c * width, width), width)]
+        return rcopy(dst, dst, h3_send.at[c], h3_recv.at[c], sib)
+
+    def step3(pair, src):
+        c = src * 2 + pair
+        rcopy(csum.at[c], rx.at[c], h2_send.at[c], h2_recv.at[c], xp).wait()
+        pre = csum[c].astype(f32) + rx[c].astype(f32) + acc_ref[:hs, 0:1]
+        act = 0.5 * pre * (1.0 + lax.erf(pre * (0.5**0.5)))
+        hid[sc, :, pl.ds(pl.multiple_of(c * width, width), width)] = act.astype(bf16)
+        hid_copy(c).start()
+
+    def hidden_step(k, carry):
+        on_chunk(k, step1)
+        on_chunk(k - 1, step2)
+        on_chunk(k - 2, step3)
+        return carry
+
+    lax.fori_loop(0, 2 * places + 2, hidden_step, 0)
+
+    def hid_wait(c, carry):
+        hid_copy(c).wait_send()
+        other = hid.at[1 - sc, :, pl.ds(pl.multiple_of(c * width, width), width)]
+        rcopy(other, other, h3_send.at[c], h3_recv.at[c], sib).wait_recv()
+        return carry
+
+    lax.fori_loop(0, 2 * (top + 1), hid_wait, 0)
+
+    all_rows = hid.shape[2]
+    out_cols = img.shape[1]
+    col_i = lax.broadcasted_iota(jnp.int32, (all_rows, out_cols), 1)
+
+    def route(q, carry):
+        pick = jnp.where(tall[:all_rows, 1:2] == col_i + q * out_cols, 1.0, 0.0).astype(bf16)
+        for half in range(2):
+            rt[q, half * hs : (half + 1) * hs] = jnp.dot(
+                hid[half], pick, preferred_element_type=f32
+            ).astype(bf16)
+        return carry
+
+    lax.fori_loop(0, top + 1, route, 0)
+
+    pieces, piece = obuf.shape[1], obuf.shape[2]
+
+    def part(q, r):
+        return dot0(w2[:, pl.ds(pl.multiple_of(r * piece, piece), piece)], rt[q])
+
+    def send_one(q, r, buf, sem, dev, has_more, from_dev):
+        acc_ref[...] = part(q, r)
+
+        @pl.when(has_more)
+        def _():
+            rcopy(obuf.at[q, r], buf.at[q, r], o_send.at[q, r], sem.at[q, r], from_dev).wait_recv()
+            acc_ref[...] += buf[q, r].astype(f32)
+
+        obuf[q, r] = acc_ref[...].astype(bf16)
+        rcopy(obuf.at[q, r], buf.at[q, r], o_send.at[q, r], sem.at[q, r], dev).start()
+
+    def out_step(k, carry):
+        delta, r = top - k // pieces, k % pieces
+
+        @pl.when(p + delta <= top)
+        def _():
+            send_one(p + delta, r, rup, u_recv, {"pool": p + 1}, p > 0, sib)
+
+        @pl.when(p - delta >= 0)
+        def _():
+            send_one(p - delta, r, rdn, d_recv, {"pool": p - 1}, p < top, sib)
+
+        return carry
+
+    lax.fori_loop(0, top * pieces, out_step, 0)
+
+    def last_step(r, squares):
+        rr = pl.ds(pl.multiple_of(r * piece, piece), piece)
+        acc_ref[...] = part(p, r) + lcols[rr, 0:1]
+
+        @pl.when(p > 0)
+        def _():
+            rcopy(obuf.at[p, r], rup.at[p, r], o_send.at[p, r], u_recv.at[p, r], sib).wait_recv()
+            acc_ref[...] += rup[p, r].astype(f32)
+
+        @pl.when(p < top)
+        def _():
+            rcopy(obuf.at[p, r], rdn.at[p, r], o_send.at[p, r], d_recv.at[p, r], sib).wait_recv()
+            acc_ref[...] += rdn[p, r].astype(f32)
+
+        res = (acc_ref[...] * live[...]).astype(bf16)
+        img[rr, :] = res
+        res = res.astype(f32)
+        return squares + jnp.sum(res * res, 0, keepdims=True)
+
+    squares = lax.fori_loop(0, pieces, last_step, jnp.zeros((1, out_cols), f32))
+    sq2[me] = jnp.broadcast_to(squares, (8, out_cols))
+    for k, (dev, t) in enumerate(peers):
+        rcopy(sq2.at[me], sq2.at[me], l_send.at[k], l_recv.at[me], dev).start()
+
+    for pair in range(2):
+        gather_drain(xall, pair, x_send, x_recv)
+        gather_drain(ctxall, pair, c_send, c_recv)
+        for k in range(3):
+            rcopy(sq.at[pair, me], sq.at[pair, me], q_send.at[pair, k], q_recv.at[pair, me], sib).wait_send()
+        for src in range(top + 1):
+            chunk = zall.at[src, pair]
+
+            @pl.when((src <= p) & (p < top))
+            def _():
+                rcopy(chunk, chunk, z_send.at[0, src, pair], z_recv.at[src, pair], sib).wait_send()
+
+            @pl.when((src >= p) & (p > 0))
+            def _():
+                rcopy(chunk, chunk, z_send.at[1, src, pair], z_recv.at[src, pair], sib).wait_send()
+
+    for k in range(3):
+        rcopy(sall.at[me], sall.at[me], s_send.at[k], s_recv.at[me], sib).wait_send()
+        rcopy(pw.at[me], pwall.at[me], w_send.at[k], w_recv.at[me], sib).wait_send()
+    for q in range(top + 1):
+
+        @pl.when(q != p)
+        def _():
+            for r in range(pieces):
+                rcopy(obuf.at[q, r], rup.at[q, r], o_send.at[q, r], u_recv.at[q, r], sib).wait_send()
+
+    for k, (dev, t) in enumerate(peers):
+        rcopy(sq2.at[t], sq2.at[t], l_send.at[k], l_recv.at[t], dev).wait()
+    squares = sq2[0, 0:1] + sq2[1, 0:1] + sq2[2, 0:1] + sq2[3, 0:1]
+    inv = lax.rsqrt(squares / model_width + EPSILON)
+
+    def norm_step(r, carry):
+        rr = pl.ds(pl.multiple_of(r * piece, piece), piece)
+        nrm[rr, :] = (img[rr, :].astype(f32) * inv * lcols[rr, 1:2]).astype(bf16)
+        return carry
+
+    lax.fori_loop(0, pieces, norm_step, 0)
+
+
+def fused_shards(
+    patches, window_ids, block_route, norm_gain, qkv_weight, qkv_bias, proj_weight, proj_bias,
+    merge_gain, w1, b1, w2, b2, llm_gain,
+):
+    f32, bf16 = jnp.float32, jnp.bfloat16
+    feat, cols = patches.shape
+    pool = lax.axis_size("pool")
+    my_pool = lax.axis_index("pool")
+    slots, block_len = window_ids.shape
+    width = qkv_weight.shape[1]
+    merged_rows = block_len // 4
+    hot_groups = max(1, pool // 16)
+    capacity = 2 * hot_groups + slots - 2
+    out_cols = capacity * merged_rows
+    goes = (block_route[:, None] == block_route[None, :]).astype(jnp.int32)
+    total = block_route.shape[0]
+    index = jnp.arange(total, dtype=jnp.int32)
+    rank = jnp.sum(jnp.where(index[None, :] < index[:, None], goes, 0), 1)
+    first = jnp.where(rank < capacity, block_route * out_cols + rank * merged_rows, -(1 << 20))
+    dest = (first[:, None] + jnp.arange(merged_rows, dtype=jnp.int32)[None, :]).reshape(-1)
+    tall = jnp.stack([window_ids.reshape(-1), dest], 1)
+    count = jnp.sum((block_route == my_pool).astype(jnp.int32))
+    live = (jnp.arange(out_cols, dtype=jnp.int32) // merged_rows < count).astype(f32)[None, :]
+    fcols = jnp.concatenate([qkv_bias.T, proj_bias[:, None], merge_gain[:, None]], 1)
+    share = w1.shape[2]
+    pad = -feat % 128
+    row = jnp.concatenate([norm_gain, jnp.zeros((pad,), f32), b1])
+    small = jnp.broadcast_to(row[None, :], (8, row.shape[0]))
+    pw = proj_weight.reshape(feat, 4, feat).transpose(1, 2, 0)
+    lcols = jnp.stack([b2, llm_gain], 1)
+    local_out = w2.shape[1]
+    hc, hs, wd = cols // 2, share // 2, cols // 8
+    n2 = 2 * pool
+    pieces = 4
+    piece = local_out // pieces
+    V, D = pltpu.VMEM, pltpu.SemaphoreType.DMA
+    scratch = [
+        V((2, 4, feat, hc), bf16), V((4, 8, row.shape[0]), f32), V((4, feat, feat), bf16),
+        V((4, feat, 1), f32), V((width, hc), bf16), V((3, feat, hc), bf16),
+        V((2, 4, feat, hc), bf16), V((pool, 2, 4, feat, wd), bf16), V((n2, 2, hs, wd), bf16),
+        V((n2, hs, wd), bf16), V((n2, hs, wd), bf16), V((n2, hs, wd), bf16),
+        V((2, hs, n2 * wd), bf16), V((pool, share, out_cols), bf16),
+        V((pool, pieces, piece, out_cols), bf16), V((pool, pieces, piece, out_cols), bf16),
+        V((pool, pieces, piece, out_cols), bf16),
+        V((2, 4, 8, hc), f32), V((4, 8, out_cols), f32), V((piece, out_cols), f32),
+        D((2, 3)), D((2, 4)), D((2, 3)), D((2, 4)), D((3,)), D((4,)), D((3,)), D((4,)),
+        D((2, 3)), D((2, 4)), D((2, pool, 2)), D((pool, 2)),
+        D((n2,)), D((n2,)), D((n2,)), D((n2,)), D((n2,)), D((n2,)),
+        D((pool, pieces)), D((pool, pieces)), D((pool, pieces)), D((3,)), D((4,)),
+    ]
+    shape = jax.ShapeDtypeStruct((local_out, out_cols), bf16)
+    vm = pl.BlockSpec(memory_space=pltpu.VMEM)
+    return pl.pallas_call(
+        functools.partial(fused_kernel, width, local_out * 4),
+        out_shape=(shape, shape),
+        in_specs=[vm] * 11,
+        out_specs=(vm, vm),
+        scratch_shapes=scratch,
+        compiler_params=pltpu.CompilerParams(
+            collective_id=0, has_side_effects=True, vmem_limit_bytes=60 << 20
+        ),
+        name="vision_fused",
+    )(patches, window_ids, tall, fcols, small, qkv_weight, pw, w1, w2, lcols, live)
+
+
+def fused_fits(mesh):
+    return mesh.shape["tensor"] == 2 and mesh.shape["sub"] == 2 and mesh.shape["pool"] == 4
+
+
 def solution(mesh):
     placed = (
         P(("tensor", "sub"), ("groups", "pool")),
@@ -136,7 +554,7 @@
         P(("tensor", "sub")),
     )
     return jax.shard_map(
-        shards,
+        fused_shards if fused_fits(mesh) else shards,
         mesh=mesh,
         in_specs=placed,
         out_specs=(

time: 328 us -> 205 us (0.62)
  waiting for transfers between devices: 224 us -> 0 us
  Pallas kernels: 0 us -> 183 us
  blocking collectives: 22.8 us -> 0 us
  matrix products: 22.4 us -> 0 us
  other arithmetic: 22.4 us -> 5.84 us
  between operations: 14 us -> 0.68 us
  local copies, waits for them, and re-layouts: 18.3 us -> 14.8 us
    pallas_call x0 -> x1, Pallas kernels: none -> 183 us  [fused_shards(): pl.pallas_call(functools.partial(fused_kernel, width, local_out * 4), out...]
    reduce_scatter x2 -> x0, waiting for transfers between devices: 110 us -> none  [the longest x1 75.5 us: shards(): lax.psum_scatter(partial.astype(jnp.bfloat16), 'pool', scatter_dimension=...]
    all_gather x2 -> x0, waiting for transfers between devices: 80.3 us -> none  [the longest x1 53 us: shards(): merged_all = lax.all_gather(merged, 'pool', axis=2, tiled=True)]
    psum x1 -> x0, waiting for transfers between devices: 33.9 us -> none  [shards(): lax.psum(jnp.einsum('jfc,jfm->cm', w1, merged_all, preferred_element_type...]
    dot_general x7 -> x0, matrix products: 22.4 us -> none  [the longest x1 5.55 us: shards(): jnp.einsum('jfc,jfm->cm', w1, merged_all, preferred_element_type=jnp.floa...]
    psum x3 -> x0, blocking collectives: 17 us -> none  [the longest x1 5.74 us: shards(): merge_squares = lax.psum(jnp.sum(out_f * out_f, 0), ('tensor', 'sub'))]
    convert_element_type x5 -> x1, other arithmetic: 14.3 us -> 1.24 us  [fused_shards(): (jnp.arange(out_cols, dtype=jnp.int32) // merged_rows < count).astype(f32)]
    squeeze x3 -> x0, local copies, waits for them, and re-layouts: 6.21 us -> none  [the longest x1 2.45 us: shards(): qkv[0]]
  transfers between devices with their start and end apart: 5 -> 0, of which waited for: 5 -> 0; matrix products, arithmetic and copies ran while one was open for 1% -> 0% of each run, Pallas kernels for 0% -> 0%
where the time goes in v2:
time: 205 us
  Pallas kernels  183 us (89%)
  local copies, waits for them, and re-layouts  14.8 us (7%)
  other arithmetic  5.84 us (3%)
    pallas_call x1, Pallas kernels, fused_shards(): pl.pallas_call(functools.partial(fused_kernel, width, local_out * 4), out...  183 us
    unnamed x9, local copies, waits for them, and re-layouts  9.52 us

profile of v2, /device:TPU:9, one launch (start us, length us, event | category | flops | bytes accessed | tf_op | source)
XLA Modules:
  0.0 204.7 jit_solution(9010909943279133960)
XLA Ops:
  0.6 0.0 copy-start
  0.6 1.0 select_reduce_fusion
  1.6 1.3 fusion
  2.9 1.2 compare_convert_fusion.live
  4.2 0.7 broadcast_in_dim.32
  4.9 0.7 broadcast_in_dim.33
  5.6 0.8 pad_maximum_fusion.2
  6.3 0.7 copy.38
  7.0 0.1 iota_add_fusion
  7.1 0.1 add.38
  7.2 0.7 pad_maximum_fusion.1
  7.9 0.7 pad_maximum_fusion
  8.6 0.6 broadcast_in_dim.35.small
  9.2 0.8 copy.35.fcols
  10.1 1.0 copy.34.tall
  11.1 2.2 %copy.33 = bf16[320,1280]{0,1:T(8,128)(2,1)} copy(bf16[320,1280]{1,0:T(8,128)(2,1)} %param.20) | data formatting | bytes 1638400 | tf_op args[6]
  13.3 1.3 copy.37.lcols
  14.6 0.0 copy-done
  14.7 3.3 %copy.36.qkv_w = bf16[3,1280,320]{2,1,0:T(8,128)(2,1)} copy(bf16[3,1280,320]{1,2,0:T(8,128)(2,1)S(1)} %copy-done) | data formatting | bytes 4915200 | tf_op args[4]
  17.9 183.4 %vision_fused.1 = (bf16[2048,256]{1,0:T(8,128)(2,1)}, bf16[2048,256]{1,0:T(8,128)(2,1)}) custom-call(bf16[320,1024]{1,0:T(8,128)(2,1)} %patches.1, s32[4,256]{1,0:T(4,128)} %ids_row.1, s32[1024,2]{1,0:T(8,128)} %copy.34.tall, f32[320,5]{1,0:T(8,128)} %copy.35.fcols, f32[8,1024]{1,0:T(8,128)} %broadcast_in_dim.35.small, bf16[3,1280,320]{2,1,0:T(8,128)(2,1)} %copy.36.qkv_w, ...), custom_call_target="tpu_custom_call" | custom-call | tf_op jit(solution)/shard_map/vision_fused/pallas_call | solution.py:522
  201.4 0.0 copy-start.1
  201.4 2.4 %copy.41 = bf16[2048,256]{1,0:T(8,128)(2,1)} copy(bf16[2048,256]{1,0:T(8,128)(2,1)} %get-tuple-element.6) | data formatting | bytes 2097152
  203.7 0.0 copy-done.1
  203.7 1.0 copy.42
  (2 shorter events, 0.0 us)
Async XLA Ops:
  0.6 14.0 %copy-start = (bf16[3,1280,320]{1,2,0:T(8,128)(2,1)S(1)}, bf16[3,1280,320]{1,2,0:T(8,128)(2,1)}, u32[]{:S(2)}) copy-start(bf16[3,1280,320]{1,2,0:T(8,128)(2,1)} %param.18) | copy-start | bytes 7372804
  201.4 2.4 %copy-start.1 = (bf16[2048,256]{1,0:T(8,128)(2,1)S(1)}, bf16[2048,256]{1,0:T(8,128)(2,1)}, u32[]{:S(2)}) copy-start(bf16[2048,256]{1,0:T(8,128)(2,1)} %get-tuple-element.7) | copy-start | bytes 3145732

commit v3 on v2

--- a/solution.py
+++ b/solution.py
@@ -123,8 +123,9 @@
 
 
 def fused_kernel(
-    vision_width, model_width, patches, ids_row, tall, fcols, small, qkv_w, pw, w1, w2, lcols, live,
-    img, nrm,
+    vision_width, model_width, patches, ids_row, routes, norm_gain, qkv_bias, proj_w, proj_bias,
+    merge_gain, b1, b2, llm_gain, qkv_hbm, w1_hbm, w2_hbm,
+    img, nrm, qkv_w, w1, w2, pw, fcols, lcols, id_col, picks, load_sem,
     xall, sall, pwall, gcol, xin, qkv, ctxall, zall, pbuf, rsib, csum, rx, hid, rt, obuf, rup, rdn,
     sq, sq2, acc_ref,
     x_send, x_recv, c_send, c_recv, s_send, s_recv, w_send, w_recv, q_send, q_recv,
@@ -138,6 +139,12 @@
     heads = feat // HDIM
     share = w1.shape[2]
     hs = share // 2
+    loads = [
+        pltpu.make_async_copy(a, b, load_sem.at[k])
+        for k, (a, b) in enumerate(((qkv_hbm, qkv_w), (w1_hbm, w1), (w2_hbm, w2)))
+    ]
+    for load in loads:
+        load.start()
     p, tx, sc = lax.axis_index("pool"), lax.axis_index("tensor"), lax.axis_index("sub")
     me, xt, st, dt = tx * 2 + sc, (1 - tx) * 2 + sc, tx * 2 + 1 - sc, (1 - tx) * 2 + 1 - sc
     xp, sib, diag = {"tensor": 1 - tx}, {"sub": 1 - sc}, {"tensor": 1 - tx, "sub": 1 - sc}
@@ -167,8 +174,9 @@
 
     for pair in range(2):
         xall[pair, me] = patches[:, pair * half_cols : (pair + 1) * half_cols]
-    sall[me] = small[...]
-    pwall[me] = pw[me]
+    base = sall.shape[2] - share
+    sall[me, 0:1, :feat] = norm_gain[...]
+    sall[me, 0:1, base:] = b1[...]
     pl.semaphore_wait(barrier, 3 + (p + top - 1) // top + (2 * top - p - 1) // top)
 
     def gather_start(buf, pair, ssem, rsem):
@@ -193,15 +201,57 @@
         rcopy(sall.at[me], sall.at[me], s_send.at[k], s_recv.at[me], dev).start()
     gather_start(xall, 0, x_send, x_recv)
     gather_start(xall, 1, x_send, x_recv)
+    for t in range(4):
+        pw[t] = proj_w[:, t * feat : (t + 1) * feat]
+    pwall[me] = pw[me]
     for k, (dev, t) in enumerate(peers):
         rcopy(pw.at[t], pwall.at[me], w_send.at[k], w_recv.at[me], dev).start()
+
+    def to_column(row):
+        size = row.shape[1]
+        r = lax.broadcasted_iota(jnp.int32, (size, size), 0)
+        c = lax.broadcasted_iota(jnp.int32, (size, size), 1)
+        return jnp.sum(jnp.where(r == c, row, 0.0), 1, keepdims=True)
+
+    for c in range(3):
+        fcols[c] = to_column(qkv_bias[c : c + 1])
+    fcols[3] = to_column(proj_bias[...])
+    fcols[4] = to_column(merge_gain[...])
+    for b in range(blocks):
+        id_col[b] = to_column(ids_row[b : b + 1].astype(f32))
+    pieces, piece = obuf.shape[1], obuf.shape[2]
+    for r in range(pieces):
+        lcols[0, r * piece : (r + 1) * piece] = to_column(b2[:, r * piece : (r + 1) * piece])
+        lcols[1, r * piece : (r + 1) * piece] = to_column(llm_gain[:, r * piece : (r + 1) * piece])
+
+    out_cols = img.shape[1]
+    merged_rows = block_len // 4
+    total_blocks = routes.shape[0]
+    r_i = lax.broadcasted_iota(jnp.int32, (merged_rows, out_cols), 0)
+    c_i = lax.broadcasted_iota(jnp.int32, (merged_rows, out_cols), 1)
+    count = 0
+    for n in range(total_blocks):
+        route_n = routes[n]
+        count += jnp.where(route_n == p, 1, 0)
+        rank = 0
+        for earlier in range(n):
+            rank += jnp.where(routes[earlier] == route_n, 1, 0)
+        first = jnp.where(
+            rank < out_cols // merged_rows, route_n * out_cols + rank * merged_rows, -(1 << 20)
+        )
+        for q in range(top + 1):
+            picks[q, n * merged_rows : (n + 1) * merged_rows] = jnp.where(
+                r_i + (first - q * out_cols) == c_i, 1.0, 0.0
+            ).astype(bf16)
+    lane = lax.broadcasted_iota(jnp.int32, (1, out_cols), 1)
+    live = jnp.where(lane < count * merged_rows, 1.0, 0.0)
+
     for k, (dev, t) in enumerate(peers):
         rcopy(sall.at[t], sall.at[t], s_send.at[k], s_recv.at[t], dev).wait_recv()
 
-    rows = lax.broadcasted_iota(jnp.int32, (feat, feat), 0)
-    lanes = lax.broadcasted_iota(jnp.int32, (feat, feat), 1)
     for t in range(4):
-        gcol[t] = jnp.sum(jnp.where(rows == lanes, sall[t, 0:1, :feat], 0.0), 1, keepdims=True)
+        gcol[t] = to_column(sall[t, 0:1, :feat])
+    loads[0].wait()
 
     def dot0(a, b):
         return lax.dot_general(a, b, (((0,), (0,)), ((), ())), preferred_element_type=f32)
@@ -219,11 +269,13 @@
                 xall[pair, t].astype(f32) * inv * gcol[t]
             ).astype(bf16)
         for c in range(3):
-            qkv[c] = (dot0(qkv_w[c], xin[...]) + fcols[:, c : c + 1]).astype(bf16)
+            qkv[c] = (
+                jnp.dot(qkv_w[c], xin[...], preferred_element_type=f32) + fcols[c]
+            ).astype(bf16)
         for bb in range(per_pair):
             b = pair * per_pair + bb
             lo = bb * block_len
-            same = tall[b * block_len : (b + 1) * block_len, 0:1] == ids_row[b : b + 1, :]
+            same = id_col[b] == ids_row[b : b + 1, :].astype(f32)
 
             def head(h, carry):
                 r = pl.ds(pl.multiple_of(h * HDIM, HDIM), HDIM)
@@ -246,10 +298,10 @@
 
     for pair in range(2):
         gather_finish(ctxall, pair, c_send, c_recv)
-        total = patches[:, pair * half_cols : (pair + 1) * half_cols].astype(f32) + fcols[:, 3:4]
+        total = patches[:, pair * half_cols : (pair + 1) * half_cols].astype(f32) + fcols[3]
         for t in range(4):
             total += (
-                jnp.dot(pwall[t], ctxall[pair, t], preferred_element_type=f32)
+                dot0(pwall[t], ctxall[pair, t])
                 .astype(bf16)
                 .astype(f32)
             )
@@ -261,7 +313,7 @@
             rcopy(sq.at[pair, t], sq.at[pair, t], q_send.at[pair, k], q_recv.at[pair, t], dev).wait_recv()
         squares = sq[pair, 0, 0:1] + sq[pair, 1, 0:1] + sq[pair, 2, 0:1] + sq[pair, 3, 0:1]
         merge_in = (
-            out * lax.rsqrt(squares / vision_width + EPSILON) * fcols[:, 4:5]
+            out * lax.rsqrt(squares / vision_width + EPSILON) * fcols[4]
         ).astype(bf16)
         n_i = lax.broadcasted_iota(jnp.int32, (half_cols, half_cols // 4), 0)
         m_i = lax.broadcasted_iota(jnp.int32, (half_cols, half_cols // 4), 1)
@@ -278,14 +330,11 @@
         def _():
             rcopy(own, own, z_send.at[1, p, pair], z_recv.at[p, pair], {"pool": p - 1}).start()
 
-    rows_h = lax.broadcasted_iota(jnp.int32, (hs, hs), 0)
-    lanes_h = lax.broadcasted_iota(jnp.int32, (hs, hs), 1)
-    base = small.shape[1] - share
     b1_lo = sall[p, 0:1, base : base + hs]
     b1_hi = sall[p, 0:1, base + hs : base + share]
     b1_row = jnp.where(sc == 0, b1_lo, b1_hi)
-    b1_col = jnp.sum(jnp.where(rows_h == lanes_h, b1_row, 0.0), 1, keepdims=True)
-    acc_ref[:hs, 0:1] = b1_col
+    acc_ref[:hs, 0:1] = to_column(b1_row)
+    loads[1].wait()
 
     places = 2 * top + 1
     width = half_cols // 4
@@ -359,22 +408,17 @@
 
     lax.fori_loop(0, 2 * (top + 1), hid_wait, 0)
 
-    all_rows = hid.shape[2]
-    out_cols = img.shape[1]
-    col_i = lax.broadcasted_iota(jnp.int32, (all_rows, out_cols), 1)
+    loads[2].wait()
 
     def route(q, carry):
-        pick = jnp.where(tall[:all_rows, 1:2] == col_i + q * out_cols, 1.0, 0.0).astype(bf16)
         for half in range(2):
             rt[q, half * hs : (half + 1) * hs] = jnp.dot(
-                hid[half], pick, preferred_element_type=f32
+                hid[half], picks[q], preferred_element_type=f32
             ).astype(bf16)
         return carry
 
     lax.fori_loop(0, top + 1, route, 0)
 
-    pieces, piece = obuf.shape[1], obuf.shape[2]
-
     def part(q, r):
         return dot0(w2[:, pl.ds(pl.multiple_of(r * piece, piece), piece)], rt[q])
 
@@ -406,7 +450,7 @@
 
     def last_step(r, squares):
         rr = pl.ds(pl.multiple_of(r * piece, piece), piece)
-        acc_ref[...] = part(p, r) + lcols[rr, 0:1]
+        acc_ref[...] = part(p, r) + lcols[0, rr]
 
         @pl.when(p > 0)
         def _():
@@ -418,7 +462,7 @@
             rcopy(obuf.at[p, r], rdn.at[p, r], o_send.at[p, r], d_recv.at[p, r], sib).wait_recv()
             acc_ref[...] += rdn[p, r].astype(f32)
 
-        res = (acc_ref[...] * live[...]).astype(bf16)
+        res = (acc_ref[...] * live).astype(bf16)
         img[rr, :] = res
         res = res.astype(f32)
         return squares + jnp.sum(res * res, 0, keepdims=True)
@@ -461,7 +505,7 @@
 
     def norm_step(r, carry):
         rr = pl.ds(pl.multiple_of(r * piece, piece), piece)
-        nrm[rr, :] = (img[rr, :].astype(f32) * inv * lcols[rr, 1:2]).astype(bf16)
+        nrm[rr, :] = (img[rr, :].astype(f32) * inv * lcols[1, rr]).astype(bf16)
         return carry
 
     lax.fori_loop(0, pieces, norm_step, 0)
@@ -474,37 +518,27 @@
     f32, bf16 = jnp.float32, jnp.bfloat16
     feat, cols = patches.shape
     pool = lax.axis_size("pool")
-    my_pool = lax.axis_index("pool")
     slots, block_len = window_ids.shape
     width = qkv_weight.shape[1]
     merged_rows = block_len // 4
     hot_groups = max(1, pool // 16)
     capacity = 2 * hot_groups + slots - 2
     out_cols = capacity * merged_rows
-    goes = (block_route[:, None] == block_route[None, :]).astype(jnp.int32)
-    total = block_route.shape[0]
-    index = jnp.arange(total, dtype=jnp.int32)
-    rank = jnp.sum(jnp.where(index[None, :] < index[:, None], goes, 0), 1)
-    first = jnp.where(rank < capacity, block_route * out_cols + rank * merged_rows, -(1 << 20))
-    dest = (first[:, None] + jnp.arange(merged_rows, dtype=jnp.int32)[None, :]).reshape(-1)
-    tall = jnp.stack([window_ids.reshape(-1), dest], 1)
-    count = jnp.sum((block_route == my_pool).astype(jnp.int32))
-    live = (jnp.arange(out_cols, dtype=jnp.int32) // merged_rows < count).astype(f32)[None, :]
-    fcols = jnp.concatenate([qkv_bias.T, proj_bias[:, None], merge_gain[:, None]], 1)
     share = w1.shape[2]
     pad = -feat % 128
-    row = jnp.concatenate([norm_gain, jnp.zeros((pad,), f32), b1])
-    small = jnp.broadcast_to(row[None, :], (8, row.shape[0]))
-    pw = proj_weight.reshape(feat, 4, feat).transpose(1, 2, 0)
-    lcols = jnp.stack([b2, llm_gain], 1)
+    row_len = feat + pad + share
     local_out = w2.shape[1]
     hc, hs, wd = cols // 2, share // 2, cols // 8
     n2 = 2 * pool
     pieces = 4
     piece = local_out // pieces
     V, D = pltpu.VMEM, pltpu.SemaphoreType.DMA
+    total = block_route.shape[0]
     scratch = [
-        V((2, 4, feat, hc), bf16), V((4, 8, row.shape[0]), f32), V((4, feat, feat), bf16),
+        V((3, feat, width), bf16), V(w1.shape, bf16), V(w2.shape, bf16), V((4, feat, feat), bf16),
+        V((5, feat, 1), f32), V((2, local_out, 1), f32), V((slots, block_len, 1), f32),
+        V((pool, total * merged_rows, out_cols), bf16), D((3,)),
+        V((2, 4, feat, hc), bf16), V((4, 8, row_len), f32), V((4, feat, feat), bf16),
         V((4, feat, 1), f32), V((width, hc), bf16), V((3, feat, hc), bf16),
         V((2, 4, feat, hc), bf16), V((pool, 2, 4, feat, wd), bf16), V((n2, 2, hs, wd), bf16),
         V((n2, hs, wd), bf16), V((n2, hs, wd), bf16), V((n2, hs, wd), bf16),
@@ -522,14 +556,20 @@
     return pl.pallas_call(
         functools.partial(fused_kernel, width, local_out * 4),
         out_shape=(shape, shape),
-        in_specs=[vm] * 11,
+        in_specs=[vm, vm, pl.BlockSpec(memory_space=pltpu.SMEM)]
+        + [vm] * 8
+        + [pl.BlockSpec(memory_space=pl.ANY)] * 3,
         out_specs=(vm, vm),
         scratch_shapes=scratch,
         compiler_params=pltpu.CompilerParams(
             collective_id=0, has_side_effects=True, vmem_limit_bytes=60 << 20
         ),
         name="vision_fused",
-    )(patches, window_ids, tall, fcols, small, qkv_weight, pw, w1, w2, lcols, live)
+    )(
+        patches, window_ids, block_route, norm_gain[None, :], qkv_bias, proj_weight,
+        proj_bias[None, :], merge_gain[None, :], b1[None, :], b2[None, :], llm_gain[None, :],
+        qkv_weight.transpose(0, 2, 1), w1, w2,
+    )
 
 
 def fused_fits(mesh):

time: 205 us -> 190 us (0.927)
  local copies, waits for them, and re-layouts: 14.8 us -> 8.31 us
  other arithmetic: 5.84 us -> 0 us
  Pallas kernels: 183 us -> 180 us
    unnamed x9 -> x4, local copies, waits for them, and re-layouts: 9.52 us -> 3.32 us
    broadcast_in_dim x4, local copies, waits for them, and re-layouts: 1.98 us -> 4.99 us  [the longest x1 1.28 us: fused_shards(): proj_bias[None, :]]
    pallas_call x1, Pallas kernels: 183 us -> 180 us  [fused_shards(): pl.pallas_call(functools.partial(fused_kernel, width, local_out * 4), out...]
    another operation x2 -> x0, local copies, waits for them, and re-layouts: 2.38 us -> none  [the longest x1 1.35 us: fused_shards(): lcols = jnp.stack([b2, llm_gain], 1)]
    reduce_sum x2 -> x0, other arithmetic: 2.3 us -> none  [the longest x1 1.3 us: fused_shards(): count = jnp.sum((block_route == my_pool).astype(jnp.int32))]
where the time goes in v3:
time: 190 us; the launch traced here: 189 us
  Pallas kernels  180 us (95%)
  local copies, waits for them, and re-layouts  8.31 us (4%)
    pallas_call x1, Pallas kernels, fused_shards(): pl.pallas_call(functools.partial(fused_kernel, width, local_out * 4), out...  180 us

profile of v3, /device:TPU:9, one launch (start us, length us, event | category | flops | bytes accessed | tf_op | source)
XLA Modules:
  0.0 189.4 jit_solution(783974491894640416)
XLA Ops:
  0.6 1.2 broadcast_in_dim.18.norm_gain
  1.9 1.3 broadcast_in_dim.19.proj_bias
  3.2 1.2 broadcast_in_dim.20.merge_gain
  4.4 1.3 broadcast_in_dim.21.b1
  5.6 180.4 %vision_fused.1 = (bf16[2048,256]{1,0:T(8,128)(2,1)}, bf16[2048,256]{1,0:T(8,128)(2,1)}) custom-call(bf16[320,1024]{1,0:T(8,128)(2,1)} %patches.1, s32[4,256]{1,0:T(4,128)} %ids_row.1, s32[16]{0:T(128)} %routes.1, f32[1,320]{1,0:T(1,128)} %broadcast_in_dim.18.norm_gain, f32[3,320]{1,0:T(4,128)} %qkv_bias.1, bf16[320,1280]{1,0:T(8,128)(2,1)} %proj_w.1, ...), custom_call_target="tpu_custom_call" | custom-call | tf_op jit(solution)/shard_map/vision_fused/pallas_call | solution.py:556
  186.1 0.0 copy-start
  186.1 2.4 %copy.18 = bf16[2048,256]{1,0:T(8,128)(2,1)} copy(bf16[2048,256]{1,0:T(8,128)(2,1)} %get-tuple-element.4) | data formatting | bytes 2097152
  188.4 0.0 copy-done
  188.4 1.0 copy.19
Async XLA Ops:
  186.1 2.4 %copy-start = (bf16[2048,256]{1,0:T(8,128)(2,1)S(1)}, bf16[2048,256]{1,0:T(8,128)(2,1)}, u32[]{:S(2)}) copy-start(bf16[2048,256]{1,0:T(8,128)(2,1)} %get-tuple-element.5) | copy-start | bytes 3145732

commit v4 on v3

--- a/solution.py
+++ b/solution.py
@@ -175,8 +175,8 @@
     for pair in range(2):
         xall[pair, me] = patches[:, pair * half_cols : (pair + 1) * half_cols]
     base = sall.shape[2] - share
-    sall[me, 0:1, :feat] = norm_gain[...]
-    sall[me, 0:1, base:] = b1[...]
+    sall[me, 0:1, :feat] = norm_gain[...][None, :]
+    sall[me, 0:1, base:] = b1[...][None, :]
     pl.semaphore_wait(barrier, 3 + (p + top - 1) // top + (2 * top - p - 1) // top)
 
     def gather_start(buf, pair, ssem, rsem):
@@ -215,8 +215,8 @@
 
     for c in range(3):
         fcols[c] = to_column(qkv_bias[c : c + 1])
-    fcols[3] = to_column(proj_bias[...])
-    fcols[4] = to_column(merge_gain[...])
+    fcols[3] = to_column(proj_bias[...][None, :])
+    fcols[4] = to_column(merge_gain[...][None, :])
     for b in range(blocks):
         id_col[b] = to_column(ids_row[b : b + 1].astype(f32))
     pieces, piece = obuf.shape[1], obuf.shape[2]
@@ -284,13 +284,13 @@
                 v = qkv[2, r, lo : lo + block_len]
                 scores = jnp.where(same, dot0(k, q) * HDIM ** (-0.5), -1e30)
                 e = jnp.exp(scores - jnp.max(scores, 0, keepdims=True))
-                a = (e / jnp.sum(e, 0, keepdims=True)).astype(bf16)
+                a = (e * (1.0 / jnp.sum(e, 0, keepdims=True))).astype(bf16)
                 ctxall[pair, me, r, lo : lo + block_len] = jnp.dot(
                     v, a, preferred_element_type=f32
                 ).astype(bf16)
                 return carry
 
-            lax.fori_loop(0, heads, head, 0)
+            lax.fori_loop(0, heads, head, 0, unroll=True)
         gather_start(ctxall, pair, c_send, c_recv)
 
     for k, (dev, t) in enumerate(peers):
@@ -566,8 +566,8 @@
         ),
         name="vision_fused",
     )(
-        patches, window_ids, block_route, norm_gain[None, :], qkv_bias, proj_weight,
-        proj_bias[None, :], merge_gain[None, :], b1[None, :], b2[None, :], llm_gain[None, :],
+        patches, window_ids, block_route, norm_gain, qkv_bias, proj_weight,
+        proj_bias, merge_gain, b1, b2[None, :], llm_gain[None, :],
         qkv_weight.transpose(0, 2, 1), w1, w2,
     )
 

time: 190 us -> 185 us (0.974)
  local copies, waits for them, and re-layouts: 8.31 us -> 3.32 us
    broadcast_in_dim x4 -> x0, local copies, waits for them, and re-layouts: 4.99 us -> none  [the longest x1 1.28 us: fused_shards(): proj_bias[None, :]]
where the time goes in v4:
time: 185 us; the launch traced here: 184 us
  Pallas kernels  180 us (97%)
  local copies, waits for them, and re-layouts  3.32 us (2%)
    pallas_call x1, Pallas kernels, fused_shards(): pl.pallas_call(functools.partial(fused_kernel, width, local_out * 4), out...  180 us

profile of v4, /device:TPU:9, one launch (start us, length us, event | category | flops | bytes accessed | tf_op | source)
XLA Modules:
  0.0 184.4 jit_solution(9301252696961684238)
XLA Ops:
  0.6 180.5 %vision_fused.1 = (bf16[2048,256]{1,0:T(8,128)(2,1)}, bf16[2048,256]{1,0:T(8,128)(2,1)}) custom-call(bf16[320,1024]{1,0:T(8,128)(2,1)} %patches.1, s32[4,256]{1,0:T(4,128)} %ids_row.1, s32[16]{0:T(128)} %routes.1, f32[320]{0:T(512)} %norm_gain.1, f32[3,320]{1,0:T(4,128)} %qkv_bias.1, bf16[320,1280]{1,0:T(8,128)(2,1)} %proj_w.1, f32[320]{0:T(512)} %proj_bias.1, ...), custom_call_target="tpu_custom_call" | custom-call | tf_op jit(solution)/shard_map/vision_fused/pallas_call | solution.py:556
  181.1 0.0 copy-start
  181.1 2.4 %copy.18 = bf16[2048,256]{1,0:T(8,128)(2,1)} copy(bf16[2048,256]{1,0:T(8,128)(2,1)} %get-tuple-element.4) | data formatting | bytes 2097152
  183.5 0.0 copy-done
  183.5 1.0 copy.19
Async XLA Ops:
  181.1 2.4 %copy-start = (bf16[2048,256]{1,0:T(8,128)(2,1)S(1)}, bf16[2048,256]{1,0:T(8,128)(2,1)}, u32[]{:S(2)}) copy-start(bf16[2048,256]{1,0:T(8,128)(2,1)} %get-tuple-element.5) | copy-start | bytes 3145732
